TPU v7x, 32 devices: a whole 2x2x4 slice. The times are simulated.
32 devices in a mesh: dp: 4 (over y, x), fsdp: 8 (over z, core).
Axes of the slice: x: 2, y: 2, z: 4, core: 2. Of those that a mesh axis runs over, the one named last changes fastest.
Arguments:
- latents: bfloat16 [128, 1024], P(None, ('dp', 'fsdp')), may hold values from -6 to 6
- gain_q: bfloat16 [1024], P(('dp', 'fsdp')), may hold values from 0.5 to 1.5
- gain_kv: bfloat16 [1024], P(('dp', 'fsdp')), may hold values from 0.5 to 1.5
- w_q: bfloat16 [1024, 1024], P(('dp', 'fsdp')), may hold values from -0.1875 to 0.1875
- w_k: bfloat16 [1024, 1024], P(('dp', 'fsdp')), may hold values from -0.1875 to 0.1875
- w_v: bfloat16 [1024, 1024], P(('dp', 'fsdp')), may hold values from -0.1875 to 0.1875
- w_o: bfloat16 [1024, 1024], P(('dp', 'fsdp')), may hold values from -0.75 to 0.75
- gain_s: bfloat16 [1024], P(('dp', 'fsdp')), may hold values from 0.5 to 1.5
- s_q: bfloat16 [1024, 1024], P(('dp', 'fsdp')), may hold values from -0.1875 to 0.1875
- s_k: bfloat16 [1024, 1024], P(('dp', 'fsdp')), may hold values from -0.1875 to 0.1875
- s_v: bfloat16 [1024, 1024], P(('dp', 'fsdp')), may hold values from -0.1875 to 0.1875
- s_o: bfloat16 [1024, 1024], P(('dp', 'fsdp')), may hold values from -0.5 to 0.5
- gain_m: bfloat16 [1024], P(('dp', 'fsdp')), may hold values from 0.5 to 1.5
- w_up: bfloat16 [1024, 4096], P(('dp', 'fsdp')), may hold values from -0.1875 to 0.1875
- w_down: bfloat16 [4096, 1024], P(('dp', 'fsdp')), may hold values from -0.09375 to 0.09375
- points: bfloat16 [65536, 1024], P(('dp', 'fsdp')), may hold values from -6 to 6
- neighbours: int32 [128, 512], P(('dp', 'fsdp')), may hold values from 0 to 2047
- lengths: int32 [128], P(('dp', 'fsdp')), may hold values from 97 to 512, as said below
- cotangent: bfloat16 [16384, 1024], P(('dp', 'fsdp')), may hold values from -6 to 6
Outputs:
- output: bfloat16 [16384, 1024], P(('dp', 'fsdp'))
- point_grad: bfloat16 [65536, 1024], P(('dp', 'fsdp'))
- grad_latents: float32 [128, 1024], P(None, ('dp', 'fsdp'))
- grad_gain_q: float32 [1024], P(('dp', 'fsdp'))
- grad_gain_kv: float32 [1024], P(('dp', 'fsdp'))
- grad_w_q: float32 [1024, 1024], P(('dp', 'fsdp'))
- grad_w_k: float32 [1024, 1024], P(('dp', 'fsdp'))
- grad_w_v: float32 [1024, 1024], P(('dp', 'fsdp'))
- grad_w_o: float32 [1024, 1024], P(('dp', 'fsdp'))
- grad_gain_s: float32 [1024], P(('dp', 'fsdp'))
- grad_s_q: float32 [1024, 1024], P(('dp', 'fsdp'))
- grad_s_k: float32 [1024, 1024], P(('dp', 'fsdp'))
- grad_s_v: float32 [1024, 1024], P(('dp', 'fsdp'))
- grad_s_o: float32 [1024, 1024], P(('dp', 'fsdp'))
- grad_gain_m: float32 [1024], P(('dp', 'fsdp'))
- grad_w_up: float32 [1024, 4096], P(('dp', 'fsdp'))
- grad_w_down: float32 [4096, 1024], P(('dp', 'fsdp'))
Inputs may be any that keep to these rules, and one draw needn't show every extreme that they name: Group g reads point (g // 4) * 2048 + neighbours[g, j] of its own block. The first lengths[g] neighbour slots of group g are live; some group has all 512.
All inputs are finite; a program needn't handle non-finite values.
Results may differ from a plain program's by a relative error of at most 0.019.
Values may be sent and summed in bfloat16 or wider, within the bound.
A program may use at most 256 MiB of HBM per device.

v0:
```python
import jax
import jax.numpy as jnp
from jax import lax
from jax.sharding import PartitionSpec as P

HEADS = 8
HEAD = 128
D = 1024
FF = 4096
LAT = 128
NEIGH = 512


EPSILON = 1e-05
MASK_FILL = -1e30
LANES = 128


def layer_norm(row_data, gain_vec):
    row_mean = jnp.mean(row_data, axis=-1, keepdims=True)
    centred = row_data - row_mean
    spread = jnp.mean(centred * centred, axis=-1, keepdims=True)
    return centred * lax.rsqrt(spread + EPSILON) * gain_vec


def gelu_tanh(values):
    inner = 0.7978845608028654 * (values + 0.044715 * values * values * values)
    return 0.5 * values * (1.0 + jnp.tanh(inner))


def dot_fwd(left_op, right_op):
    return jnp.dot(left_op, right_op, preferred_element_type=jnp.float32)


def dot_back(grad_op, weight_op):
    return lax.dot_general(
        grad_op, weight_op, (((1,), (1,)), ((), ())), preferred_element_type=jnp.float32
    )


def outer_sum(left_op, right_op):
    return lax.dot_general(
        left_op, right_op, (((0,), (0,)), ((), ())), preferred_element_type=jnp.float32
    )


def to_lanes(matrix):
    return matrix.reshape(-1, LANES)


def from_lanes(flat_rows, width):
    return flat_rows.reshape(-1, width)


def attend_probs(query_g, keys_g, live_mask):
    score_scale = query_g.shape[-1] ** (-0.5)
    scores = (
        jnp.einsum("gqhe,gkhe->ghqk", query_g, keys_g, preferred_element_type=jnp.float32)
        * score_scale
    )
    if live_mask is not None:
        scores = jnp.where(live_mask, scores, MASK_FILL)
    top_score = jnp.max(scores, axis=-1, keepdims=True)
    exp_terms = jnp.exp(scores - top_score)
    return exp_terms / jnp.sum(exp_terms, axis=-1, keepdims=True)


def attend(query_g, keys_g, values_g, live_mask):
    probs_low = attend_probs(query_g, keys_g, live_mask).astype(jnp.bfloat16)
    return jnp.einsum(
        "ghqk,gkhe->gqhe", probs_low, values_g, preferred_element_type=jnp.float32
    ).astype(jnp.bfloat16)


def attend_back(query_g, keys_g, values_g, live_mask, mix_grad):
    score_scale = query_g.shape[-1] ** (-0.5)
    probs = attend_probs(query_g, keys_g, live_mask)
    probs_low = probs.astype(jnp.bfloat16)
    prob_grad = jnp.einsum(
        "gqhe,gkhe->ghqk", mix_grad, values_g, preferred_element_type=jnp.float32
    )
    score_grad = (probs * (prob_grad - jnp.sum(probs * prob_grad, axis=-1, keepdims=True))).astype(
        jnp.bfloat16
    )
    query_grad = (
        jnp.einsum("ghqk,gkhe->gqhe", score_grad, keys_g, preferred_element_type=jnp.float32)
        * score_scale
    )
    key_grad = (
        jnp.einsum("ghqk,gqhe->gkhe", score_grad, query_g, preferred_element_type=jnp.float32)
        * score_scale
    )
    value_grad = jnp.einsum(
        "ghqk,gqhe->gkhe", probs_low, mix_grad, preferred_element_type=jnp.float32
    )
    return (query_grad, key_grad, value_grad)


def on_device(
    latents,
    gain_q,
    gain_kv,
    w_q,
    w_k,
    w_v,
    w_o,
    gain_s,
    s_q,
    s_k,
    s_v,
    s_o,
    gain_m,
    w_up,
    w_down,
    points,
    neighbours,
    lengths,
    cotangent,
):
    attn_set = (
        lax.all_gather(latents, ("dp", "fsdp"), axis=1, tiled=True),
        lax.all_gather(gain_q, ("dp", "fsdp"), axis=0, tiled=True),
        lax.all_gather(gain_kv, ("dp", "fsdp"), axis=0, tiled=True),
        lax.all_gather(w_q, ("dp", "fsdp"), axis=0, tiled=True),
        lax.all_gather(w_k, ("dp", "fsdp"), axis=0, tiled=True),
        lax.all_gather(w_v, ("dp", "fsdp"), axis=0, tiled=True),
        lax.all_gather(w_o, ("dp", "fsdp"), axis=0, tiled=True),
        lax.all_gather(gain_s, ("dp", "fsdp"), axis=0, tiled=True),
        lax.all_gather(s_q, ("dp", "fsdp"), axis=0, tiled=True),
        lax.all_gather(s_k, ("dp", "fsdp"), axis=0, tiled=True),
        lax.all_gather(s_v, ("dp", "fsdp"), axis=0, tiled=True),
        lax.all_gather(s_o, ("dp", "fsdp"), axis=0, tiled=True),
    )
    (
        lat_full,
        gq_full,
        gkv_full,
        wq_full,
        wk_full,
        wv_full,
        wo_full,
        gs_full,
        sq_full,
        sk_full,
        sv_full,
        so_full,
    ) = attn_set
    groups = neighbours.shape[0]
    point_count = points.shape[0]
    row_count = groups * LAT
    lat_float = lat_full.astype(jnp.float32)
    h_q = layer_norm(lat_float, gq_full.astype(jnp.float32)).astype(jnp.bfloat16)
    query = dot_fwd(h_q, wq_full).astype(jnp.bfloat16)
    point_float = points.astype(jnp.float32)
    h_p = layer_norm(point_float, gkv_full.astype(jnp.float32)).astype(jnp.bfloat16)
    key_pts = dot_fwd(h_p, wk_full).astype(jnp.bfloat16)
    value_pts = dot_fwd(h_p, wv_full).astype(jnp.bfloat16)
    flat_index = neighbours.reshape(-1)
    keys_g = jnp.take(key_pts, flat_index, axis=0).reshape(groups, NEIGH, HEADS, HEAD)
    values_g = jnp.take(value_pts, flat_index, axis=0).reshape(groups, NEIGH, HEADS, HEAD)
    live_mask = (jnp.arange(NEIGH, dtype=jnp.int32)[None, :] < lengths[:, None])[:, None, None, :]
    query_g = jnp.broadcast_to(query.reshape(1, LAT, HEADS, HEAD), (groups, LAT, HEADS, HEAD))
    cross_mix = attend(query_g, keys_g, values_g, live_mask).reshape(row_count, D)
    cross_out = dot_fwd(cross_mix, wo_full)
    resid_one = (lat_float[None] + cross_out.reshape(groups, LAT, D)).reshape(row_count, D)
    h_s = layer_norm(resid_one, gs_full.astype(jnp.float32)).astype(jnp.bfloat16)
    self_q = dot_fwd(h_s, sq_full).astype(jnp.bfloat16).reshape(groups, LAT, HEADS, HEAD)
    self_k = dot_fwd(h_s, sk_full).astype(jnp.bfloat16).reshape(groups, LAT, HEADS, HEAD)
    self_v = dot_fwd(h_s, sv_full).astype(jnp.bfloat16).reshape(groups, LAT, HEADS, HEAD)
    self_mix = attend(self_q, self_k, self_v, None).reshape(row_count, D)
    resid_two = resid_one + dot_fwd(self_mix, so_full)
    mlp_set = (
        lax.all_gather(gain_m, ("dp", "fsdp"), axis=0, tiled=True),
        lax.all_gather(w_up, ("dp", "fsdp"), axis=0, tiled=True),
        lax.all_gather(w_down, ("dp", "fsdp"), axis=0, tiled=True),
    )
    gm_full, wup_full, wdown_full = mlp_set
    h_m = layer_norm(resid_two, gm_full.astype(jnp.float32)).astype(jnp.bfloat16)
    up_vals = dot_fwd(h_m, wup_full)
    act_vals = gelu_tanh(up_vals).astype(jnp.bfloat16)
    output = (resid_two + dot_fwd(act_vals, wdown_full)).astype(jnp.bfloat16)
    attn_back = (
        lax.all_gather(latents, ("dp", "fsdp"), axis=1, tiled=True),
        lax.all_gather(gain_q, ("dp", "fsdp"), axis=0, tiled=True),
        lax.all_gather(gain_kv, ("dp", "fsdp"), axis=0, tiled=True),
        lax.all_gather(w_q, ("dp", "fsdp"), axis=0, tiled=True),
        lax.all_gather(w_k, ("dp", "fsdp"), axis=0, tiled=True),
        lax.all_gather(w_v, ("dp", "fsdp"), axis=0, tiled=True),
        lax.all_gather(w_o, ("dp", "fsdp"), axis=0, tiled=True),
        lax.all_gather(gain_s, ("dp", "fsdp"), axis=0, tiled=True),
        lax.all_gather(s_q, ("dp", "fsdp"), axis=0, tiled=True),
        lax.all_gather(s_k, ("dp", "fsdp"), axis=0, tiled=True),
        lax.all_gather(s_v, ("dp", "fsdp"), axis=0, tiled=True),
        lax.all_gather(s_o, ("dp", "fsdp"), axis=0, tiled=True),
    )
    mlp_back = (
        lax.all_gather(gain_m, ("dp", "fsdp"), axis=0, tiled=True),
        lax.all_gather(w_up, ("dp", "fsdp"), axis=0, tiled=True),
        lax.all_gather(w_down, ("dp", "fsdp"), axis=0, tiled=True),
    )
    (
        lat_back,
        gq_back,
        gkv_back,
        wq_back,
        wk_back,
        wv_back,
        wo_back,
        gs_back,
        sq_back,
        sk_back,
        sv_back,
        so_back,
    ) = attn_back
    gm_back, wup_back, wdown_back = mlp_back
    grad_three = cotangent.astype(jnp.float32)
    down_in = grad_three.astype(jnp.bfloat16)
    grad_wdown = outer_sum(act_vals, down_in)
    act_grad = dot_back(down_in, wdown_back)
    gelu_value, gelu_pull = jax.vjp(gelu_tanh, up_vals)
    up_grad = gelu_pull(act_grad)[0].astype(jnp.bfloat16)
    grad_wup = outer_sum(h_m, up_grad)
    hm_grad = dot_back(up_grad, wup_back)
    norm_value, norm_pull = jax.vjp(layer_norm, resid_two, gm_back.astype(jnp.float32))
    resid_pull, grad_gm = norm_pull(hm_grad)
    grad_two = grad_three + resid_pull
    mlp_sums = (
        lax.psum_scatter(grad_gm, ("dp", "fsdp"), scatter_dimension=0, tiled=True),
        lax.psum_scatter(to_lanes(grad_wup), ("dp", "fsdp"), scatter_dimension=0, tiled=True),
        lax.psum_scatter(to_lanes(grad_wdown), ("dp", "fsdp"), scatter_dimension=0, tiled=True),
    )
    two_low = grad_two.astype(jnp.bfloat16)
    grad_so = outer_sum(self_mix, two_low)
    self_grad = dot_back(two_low, so_back).astype(jnp.bfloat16).reshape(groups, LAT, HEADS, HEAD)
    sq_grad, sk_grad, sv_grad = attend_back(self_q, self_k, self_v, None, self_grad)
    sq_low = sq_grad.reshape(row_count, D).astype(jnp.bfloat16)
    sk_low = sk_grad.reshape(row_count, D).astype(jnp.bfloat16)
    sv_low = sv_grad.reshape(row_count, D).astype(jnp.bfloat16)
    grad_sq = outer_sum(h_s, sq_low)
    grad_sk = outer_sum(h_s, sk_low)
    grad_sv = outer_sum(h_s, sv_low)
    hs_grad = dot_back(sq_low, sq_back) + dot_back(sk_low, sk_back) + dot_back(sv_low, sv_back)
    norm_value, norm_pull = jax.vjp(layer_norm, resid_one, gs_back.astype(jnp.float32))
    resid_pull, grad_gs = norm_pull(hs_grad)
    grad_one = grad_two + resid_pull
    one_low = grad_one.astype(jnp.bfloat16)
    grad_wo = outer_sum(cross_mix, one_low)
    cross_grad = dot_back(one_low, wo_back).astype(jnp.bfloat16).reshape(groups, LAT, HEADS, HEAD)
    cq_grad, ck_grad, cv_grad = attend_back(query_g, keys_g, values_g, live_mask, cross_grad)
    query_low = jnp.sum(cq_grad, axis=0).reshape(LAT, D).astype(jnp.bfloat16)
    pair_rows = jnp.concatenate(
        (ck_grad.reshape(groups * NEIGH, D), cv_grad.reshape(groups * NEIGH, D)), axis=1
    )
    pair_points = jnp.zeros((point_count, 2 * D), jnp.float32).at[flat_index].add(pair_rows)
    key_low = pair_points[:, :D].astype(jnp.bfloat16)
    value_low = pair_points[:, D:].astype(jnp.bfloat16)
    grad_wq = outer_sum(h_q, query_low)
    grad_wk = outer_sum(h_p, key_low)
    grad_wv = outer_sum(h_p, value_low)
    hq_grad = dot_back(query_low, wq_back)
    lat_value = lat_back.astype(jnp.float32)
    norm_value, norm_pull = jax.vjp(layer_norm, lat_value, gq_back.astype(jnp.float32))
    lat_pull, grad_gq = norm_pull(hq_grad)
    grad_lat = jnp.sum(grad_one.reshape(groups, LAT, D), axis=0) + lat_pull
    hp_grad = dot_back(key_low, wk_back) + dot_back(value_low, wv_back)
    norm_value, norm_pull = jax.vjp(layer_norm, point_float, gkv_back.astype(jnp.float32))
    point_pull, grad_gkv = norm_pull(hp_grad)
    point_grad = point_pull.astype(jnp.bfloat16)
    attn_sums = (
        lax.psum_scatter(grad_lat, ("dp", "fsdp"), scatter_dimension=1, tiled=True),
        lax.psum_scatter(grad_gq, ("dp", "fsdp"), scatter_dimension=0, tiled=True),
        lax.psum_scatter(grad_gkv, ("dp", "fsdp"), scatter_dimension=0, tiled=True),
        lax.psum_scatter(to_lanes(grad_wq), ("dp", "fsdp"), scatter_dimension=0, tiled=True),
        lax.psum_scatter(to_lanes(grad_wk), ("dp", "fsdp"), scatter_dimension=0, tiled=True),
        lax.psum_scatter(to_lanes(grad_wv), ("dp", "fsdp"), scatter_dimension=0, tiled=True),
        lax.psum_scatter(to_lanes(grad_wo), ("dp", "fsdp"), scatter_dimension=0, tiled=True),
        lax.psum_scatter(grad_gs, ("dp", "fsdp"), scatter_dimension=0, tiled=True),
        lax.psum_scatter(to_lanes(grad_sq), ("dp", "fsdp"), scatter_dimension=0, tiled=True),
        lax.psum_scatter(to_lanes(grad_sk), ("dp", "fsdp"), scatter_dimension=0, tiled=True),
        lax.psum_scatter(to_lanes(grad_sv), ("dp", "fsdp"), scatter_dimension=0, tiled=True),
        lax.psum_scatter(to_lanes(grad_so), ("dp", "fsdp"), scatter_dimension=0, tiled=True),
    )
    summed = tuple(attn_sums) + tuple(mlp_sums)
    return (
        output,
        point_grad,
        summed[0],
        summed[1],
        summed[2],
        from_lanes(summed[3], D),
        from_lanes(summed[4], D),
        from_lanes(summed[5], D),
        from_lanes(summed[6], D),
        summed[7],
        from_lanes(summed[8], D),
        from_lanes(summed[9], D),
        from_lanes(summed[10], D),
        from_lanes(summed[11], D),
        summed[12],
        from_lanes(summed[13], FF),
        from_lanes(summed[14], D),
    )


def solution(mesh):
    placed = (
        P(None, ("dp", "fsdp")),
        P(("dp", "fsdp")),
        P(("dp", "fsdp")),
        P(("dp", "fsdp"), None),
        P(("dp", "fsdp"), None),
        P(("dp", "fsdp"), None),
        P(("dp", "fsdp"), None),
        P(("dp", "fsdp")),
        P(("dp", "fsdp"), None),
        P(("dp", "fsdp"), None),
        P(("dp", "fsdp"), None),
        P(("dp", "fsdp"), None),
        P(("dp", "fsdp")),
        P(("dp", "fsdp"), None),
        P(("dp", "fsdp"), None),
        P(("dp", "fsdp"), None),
        P(("dp", "fsdp"), None),
        P(("dp", "fsdp")),
        P(("dp", "fsdp"), None),
    )
    return jax.shard_map(
        on_device,
        mesh=mesh,
        in_specs=placed,
        out_specs=(
            P(("dp", "fsdp"), None),
            P(("dp", "fsdp"), None),
            P(None, ("dp", "fsdp")),
            P(("dp", "fsdp")),
            P(("dp", "fsdp")),
            P(("dp", "fsdp"), None),
            P(("dp", "fsdp"), None),
            P(("dp", "fsdp"), None),
            P(("dp", "fsdp"), None),
            P(("dp", "fsdp")),
            P(("dp", "fsdp"), None),
            P(("dp", "fsdp"), None),
            P(("dp", "fsdp"), None),
            P(("dp", "fsdp"), None),
            P(("dp", "fsdp")),
            P(("dp", "fsdp"), None),
            P(("dp", "fsdp"), None),
        ),
        check_vma=False,
    )
```

profile of v0, /device:TPU:0, one launch (start us, length us, event | category | flops | bytes accessed | tf_op | source)
XLA Modules:
  0.0 2368.4 jit_solution(14748774609524402634)
XLA Ops:
  14.1 6.5 copy.135
  21.5 42.1 %all-reduce.9 = (bf16[1024]{0:T(1024)(128)(2,1)S(1)}, bf16[1024]{0:T(1024)(128)(2,1)S(1)}, bf16[1024]{0:T(1024)(128)(2,1)S(1)}, bf16[1024]{0:T(1024)(128)(2,1)S(1)}) all-reduce(bf16[1024]{0:T(1024)(128)(2,1)S(1)} %dynamic-update-slice, bf16[1024]{0:T(1024)(128)(2,1)S(1)} %dynamic-update-slice.1, ...), channel_id=1, replica_groups=mesh['dp'=4,'fsdp'=8] {'dp','fsdp'}, use_global_device_ids=true, to_apply=%add | all-reduce | flops 4096 | bytes 16384
  63.6 41.5 %all_gather.60 = bf16[128,1024]{0,1:T(8,128)(2,1)S(1)} all-gather(bf16[128,32]{0,1:T(8,128)(2,1)S(1)} %copy-done.66), channel_id=1, replica_groups=mesh['dp'=4,'fsdp'=8] {'dp','fsdp'}, dimensions={1}, use_global_device_ids=true | all-gather | bytes 270336 | tf_op jit(solution)/shard_map/all_gather | solution.py:121
  110.7 9.7 convolution_convert_fusion
  120.5 13.9 gather_fusion.1
  134.4 9.7 convolution_convert_fusion.1
  144.1 13.8 gather_fusion
  167.9 7.9 copy.164
  175.8 11.7 all-gather.13.cloned.1.call-done
  189.7 6.9 fusion.98
  196.6 8.9 fusion.124
  212.0 33.7 %all-gather.17.cloned.1.call-done = bf16[1024,1024]{1,0:T(8,128)(2,1)} async-done(((bf16[32,1024]{1,0:T(8,128)(2,1)}), bf16[1024,1024]{1,0:T(8,128)(2,1)}) %all-gather.17.cloned.1.call-update) | async-done | bytes 2097168 | tf_op jit(solution)/shard_map/all_gather | solution.py:127
  250.2 53.6 %all-gather.19.cloned.1.call-done = bf16[1024,1024]{1,0:T(8,128)(2,1)} async-done(((bf16[32,1024]{1,0:T(8,128)(2,1)}), bf16[1024,1024]{1,0:T(8,128)(2,1)}) %all-gather.19.cloned.1.call-update) | async-done | bytes 2097168 | tf_op jit(solution)/shard_map/all_gather | solution.py:131
  308.0 54.1 %all-gather.21.cloned.1.call-done = bf16[1024,1024]{1,0:T(8,128)(2,1)} async-done(((bf16[32,1024]{1,0:T(8,128)(2,1)}), bf16[1024,1024]{1,0:T(8,128)(2,1)}) %all-gather.21.cloned.1.call-update) | async-done | bytes 2097168 | tf_op jit(solution)/shard_map/all_gather | solution.py:129
  367.9 52.5 %all-gather.23.cloned.1.call-done = bf16[1024,1024]{1,0:T(8,128)(2,1)} async-done(((bf16[32,1024]{1,0:T(8,128)(2,1)}), bf16[1024,1024]{1,0:T(8,128)(2,1)}) %all-gather.23.cloned.1.call-update) | async-done | bytes 2097168 | tf_op jit(solution)/shard_map/all_gather | solution.py:130
  436.9 41.8 %all-gather.25.cloned.1.call-done = bf16[1024,1024]{1,0:T(8,128)(2,1)} async-done(((bf16[32,1024]{1,0:T(8,128)(2,1)}), bf16[1024,1024]{1,0:T(8,128)(2,1)}) %all-gather.25.cloned.1.call-update) | async-done | bytes 2097168 | tf_op jit(solution)/shard_map/all_gather | solution.py:132
  483.7 74.3 %all-gather.29.cloned.1.call-done = bf16[4096,1024]{1,0:T(8,128)(2,1)} async-done(((bf16[128,1024]{1,0:T(8,128)(2,1)}), bf16[4096,1024]{1,0:T(8,128)(2,1)}) %all-gather.29.cloned.1.call-update) | async-done | bytes 8388624 | tf_op jit(solution)/shard_map/all_gather | solution.py:175
  558.0 11.5 fusion.128
  569.5 67.2 %all-gather.27.cloned.1.call-done = bf16[1024,4096]{1,0:T(8,128)(2,1)} async-done(((bf16[32,4096]{1,0:T(8,128)(2,1)}), bf16[1024,4096]{1,0:T(8,128)(2,1)}) %all-gather.27.cloned.1.call-update) | async-done | bytes 8388624 | tf_op jit(solution)/shard_map/all_gather | solution.py:174
  636.8 18.9 fusion.20
  655.7 7.5 multiply_reduce_fusion.1
  698.2 7.8 multiply_reduce_fusion
  722.1 8.0 convolution_bitcast_fusion
  730.0 10.1 copy.163
  740.1 6.7 multiply_bitcast_fusion
  746.8 9.9 copy.161
  756.7 13.3 copy_bitcast_fusion
  770.0 35.2 %scatter_custom_fusion = f32[2048,2048]{1,0:T(8,128)} fusion(s32[2048]{0:T(1024)S(1)} %bitcast.217, f32[2048,1024]{1,0:T(8,128)} %get-tuple-element.130, f32[]{:T(128)} %constant.26.clone.1, f32[2048,1024]{1,0:T(8,128)} %get-tuple-element.131, f32[]{:T(128)} %constant.21.clone.1), kind=kCustom, calls=%fused_computation.5 | custom fusion | flops 8388608 | bytes 33554440 | tf_op jit(solution)/shard_map/scatter-add | solution.py:254
  805.2 7.3 convert.4
  827.3 10.1 fusion.29
  894.6 10.5 fusion.113
  905.1 18.0 reshape.418
  924.3 15.0 fusion.115
  939.4 18.0 reshape.420
  959.0 9.1 fusion.34
  968.1 8.9 fusion.16
  985.6 6.6 copy.168
  996.9 39.7 %all-reduce.8 = (f32[1024]{0:T(1024)S(1)}, f32[1024]{0:T(1024)S(1)}, f32[1024]{0:T(1024)S(1)}, f32[1024]{0:T(1024)S(1)}) all-reduce(f32[1024]{0:T(1024)S(1)} %get-tuple-element.92, f32[1024]{0:T(1024)S(1)} %get-tuple-element.86, f32[1024]{0:T(1024)S(1)} %copy-done.59, ...), channel_id=3, replica_groups=mesh['dp'=4,'fsdp'=8] {'dp','fsdp'}, use_global_device_ids=true, to_apply=%region_27.29.clone | all-reduce | flops 4096 | bytes 32768
  1039.0 11.9 add_convert_fusion.1
  1054.0 91.9 %reduce-scatter.18.cloned.1.call-done = f32[256,128]{1,0:T(8,128)} async-done(((f32[8192,128]{1,0:T(8,128)}), f32[256,128]{1,0:T(8,128)}) %reduce-scatter.18.cloned.1.call-update) | async-done | bytes 131088 | tf_op jit(solution)/shard_map/reduce_scatter | solution.py:275
  1147.5 140.2 %reduce-scatter.20.cloned.1.call-done = f32[256,128]{1,0:T(8,128)} async-done(((f32[8192,128]{1,0:T(8,128)}), f32[256,128]{1,0:T(8,128)}) %reduce-scatter.20.cloned.1.call-update) | async-done | bytes 131088 | tf_op jit(solution)/shard_map/reduce_scatter | solution.py:276
  1289.2 140.4 %reduce-scatter.22.cloned.1.call-done = f32[256,128]{1,0:T(8,128)} async-done(((f32[8192,128]{1,0:T(8,128)}), f32[256,128]{1,0:T(8,128)}) %reduce-scatter.22.cloned.1.call-update) | async-done | bytes 131088 | tf_op jit(solution)/shard_map/reduce_scatter | solution.py:278
  1431.3 139.7 %reduce-scatter.24.cloned.1.call-done = f32[256,128]{1,0:T(8,128)} async-done(((f32[8192,128]{1,0:T(8,128)}), f32[256,128]{1,0:T(8,128)}) %reduce-scatter.24.cloned.1.call-update) | async-done | bytes 131088 | tf_op jit(solution)/shard_map/reduce_scatter | solution.py:279
  1572.5 140.1 %reduce-scatter.26.cloned.1.call-done = f32[256,128]{1,0:T(8,128)} async-done(((f32[8192,128]{1,0:T(8,128)}), f32[256,128]{1,0:T(8,128)}) %reduce-scatter.26.cloned.1.call-update) | async-done | bytes 131088 | tf_op jit(solution)/shard_map/reduce_scatter | solution.py:280
  1714.3 140.4 %reduce-scatter.28.cloned.1.call-done = f32[256,128]{1,0:T(8,128)} async-done(((f32[8192,128]{1,0:T(8,128)}), f32[256,128]{1,0:T(8,128)}) %reduce-scatter.28.cloned.1.call-update) | async-done | bytes 131088 | tf_op jit(solution)/shard_map/reduce_scatter | solution.py:281
  1856.2 184.2 %reduce-scatter.30.cloned.1.call-done = f32[1024,128]{1,0:T(8,128)} async-done(((f32[32768,128]{1,0:T(8,128)}), f32[1024,128]{1,0:T(8,128)}) %reduce-scatter.30.cloned.1.call-update) | async-done | bytes 524304 | tf_op jit(solution)/shard_map/reduce_scatter | solution.py:229
  2042.4 184.6 %reduce-scatter.32.cloned.1.call-done = f32[1024,128]{1,0:T(8,128)} async-done(((f32[32768,128]{1,0:T(8,128)}), f32[1024,128]{1,0:T(8,128)}) %reduce-scatter.32.cloned.1.call-update) | async-done | bytes 524304 | tf_op jit(solution)/shard_map/reduce_scatter | solution.py:230
  2228.9 132.4 %reduce-scatter.34.cloned.1.call-done = f32[32,128]{1,0:T(8,128)} async-done(((f32[1024,128]{1,0:T(8,128)}), f32[32,128]{1,0:T(8,128)}) %reduce-scatter.34.cloned.1.call-update) | async-done | bytes 16400
  (333 shorter events, 225.0 us)
Async XLA Ops:
  7.2 103.5 %all-gather.15.cloned.1.call-start = ((), (), s32[]{:S(2)}) async-start(), calls=%async_computation.13 | async-start | bytes 2162688 | tf_op jit(solution)/shard_map/all_gather | solution.py:125
  7.9 126.4 %all-gather.11.cloned.1.call-start = ((), (), s32[]{:S(2)}) async-start(), calls=%async_computation.11 | async-start | bytes 2162688 | tf_op jit(solution)/shard_map/all_gather | solution.py:126
  8.7 178.8 %all-gather.13.cloned.1.call-start = ((), (), s32[]{:S(2)}) async-start(), calls=%async_computation.12 | async-start | bytes 2162688 | tf_op jit(solution)/shard_map/all_gather | solution.py:124
  9.4 236.2 %all-gather.17.cloned.1.call-start = ((), (), s32[]{:S(2)}) async-start(), calls=%async_computation.14 | async-start | bytes 2162688 | tf_op jit(solution)/shard_map/all_gather | solution.py:127
  10.0 293.9 %all-gather.19.cloned.1.call-start = ((), (), s32[]{:S(2)}) async-start(), calls=%async_computation.15 | async-start | bytes 2162688 | tf_op jit(solution)/shard_map/all_gather | solution.py:131
  10.6 351.5 %all-gather.21.cloned.1.call-start = ((), (), s32[]{:S(2)}) async-start(), calls=%async_computation.16 | async-start | bytes 2162688 | tf_op jit(solution)/shard_map/all_gather | solution.py:129
  11.1 409.3 %all-gather.23.cloned.1.call-start = ((), (), s32[]{:S(2)}) async-start(), calls=%async_computation.17 | async-start | bytes 2162688 | tf_op jit(solution)/shard_map/all_gather | solution.py:130
  11.9 466.9 %all-gather.25.cloned.1.call-start = ((), (), s32[]{:S(2)}) async-start(), calls=%async_computation.18 | async-start | bytes 2162688 | tf_op jit(solution)/shard_map/all_gather | solution.py:132
  12.6 545.4 %all-gather.29.cloned.1.call-start = ((), (), s32[]{:S(2)}) async-start(), calls=%async_computation.20 | async-start | bytes 8650752 | tf_op jit(solution)/shard_map/all_gather | solution.py:175
  13.4 623.4 %all-gather.27.cloned.1.call-start = ((), (), s32[]{:S(2)}) async-start(), calls=%async_computation.19 | async-start | bytes 8650752 | tf_op jit(solution)/shard_map/all_gather | solution.py:174
  14.0 1036.9 %reduce-scatter.14.cloned.1.call-start = ((), (), s32[]{:S(2)}) async-start(), calls=%async_computation.21 | async-start | bytes 4325376 | tf_op jit(solution)/shard_map/reduce_scatter | solution.py:273
  14.1 49.5 %copy-start.51 = (s32[4,512]{1,0:T(4,128)S(1)}, s32[4,512]{1,0:T(4,128)}, u32[]{:S(2)}) copy-start(s32[4,512]{1,0:T(4,128)} %param.37) | copy-start | bytes 24580
  14.1 49.5 %copy-start.66 = (bf16[128,32]{0,1:T(8,128)(2,1)S(1)}, bf16[128,32]{0,1:T(8,128)(2,1)}, u32[]{:S(2)}) copy-start(bf16[128,32]{0,1:T(8,128)(2,1)} %param.21) | copy-start | bytes 24580
  14.1 91.7 %copy-start.70 = (s32[4]{0:T(128)S(1)}, s32[4]{0:T(128)}, u32[]{:S(2)}) copy-start(s32[4]{0:T(128)} %param.38) | copy-start | bytes 52
  63.6 70.8 %copy-start.49 = (f32[1024]{0:T(1024)}, f32[1024]{0:T(1024)S(1)}, u32[]{:S(2)}) copy-start(f32[1024]{0:T(1024)S(1)} %convert_element_type.160) | copy-start | bytes 12292
  105.3 607.7 %copy-start.3 = (bf16[128,1024]{1,0:T(8,128)(2,1)}, bf16[128,1024]{1,0:T(8,128)(2,1)S(1)}, u32[]{:S(2)}) copy-start(bf16[128,1024]{1,0:T(8,128)(2,1)S(1)} %copy.134) | copy-start | bytes 786436
  105.3 607.7 %copy-start.41 = (f32[1024]{0:T(1024)}, f32[1024]{0:T(1024)S(1)}, u32[]{:S(2)}) copy-start(f32[1024]{0:T(1024)S(1)} %convert_element_type.163) | copy-start | bytes 12292
  105.4 557.8 %copy-start.60 = (f32[1024]{0:T(1024)}, f32[1024]{0:T(1024)S(1)}, u32[]{:S(2)}) copy-start(f32[1024]{0:T(1024)S(1)} %convert_element_type.178) | copy-start | bytes 12292
  105.5 607.5 %copy-start.53 = (f32[128]{0:T(128)}, f32[128]{0:T(128)S(1)}, u32[]{:S(2)}) copy-start(f32[128]{0:T(128)S(1)} %broadcast_multiply_fusion.3) | copy-start | bytes 1540
  105.8 607.2 %copy-start.62 = (f32[128]{0:T(128)}, f32[128]{0:T(128)S(1)}, u32[]{:S(2)}) copy-start(f32[128]{0:T(128)S(1)} %fusion.104) | copy-start | bytes 1540
  109.5 24.8 %copy-start.43 = (f32[2048]{0:T(1024)}, f32[2048]{0:T(1024)S(1)}, u32[]{:S(2)}) copy-start(f32[2048]{0:T(1024)S(1)} %broadcast_multiply_fusion) | copy-start | bytes 24580
  110.7 9.8 copy-start.45
  110.7 23.7 copy-start.47
  196.6 12.2 copy-start.23
  250.2 111.8 %copy-start.34 = (bf16[512,1024]{1,0:T(8,128)(2,1)}, bf16[512,1024]{1,0:T(8,128)(2,1)S(1)}, u32[]{:S(2)}) copy-start(bf16[512,1024]{1,0:T(8,128)(2,1)S(1)} %multiply_convert_fusion.6) | copy-start | bytes 3145732
  482.0 181.2 %copy-start.57 = (f32[512]{0:T(512)}, f32[512]{0:T(512)S(1)}, u32[]{:S(2)}) copy-start(f32[512]{0:T(512)S(1)} %broadcast_multiply_fusion.1) | copy-start | bytes 6148
  483.7 179.5 %copy-start.64 = (f32[512]{0:T(512)}, f32[512]{0:T(512)S(1)}, u32[]{:S(2)}) copy-start(f32[512]{0:T(512)S(1)} %fusion.102) | copy-start | bytes 6148
  636.8 18.9 copy-start.15
  636.8 18.9 copy-start.71
  720.8 331.6 %reduce-scatter.16.cloned.1.call-start = ((), (), s32[]{:S(2)}) async-start(), calls=%async_computation.22 | async-start | bytes 4325376 | tf_op jit(solution)/shard_map/reduce_scatter | solution.py:274
  730.0 10.1 copy-start.20
  805.2 10.6 copy-start.1
  805.2 10.6 copy-start.44
  805.2 10.6 copy-start.48
  805.2 10.6 copy-start.50
  827.0 318.9 %reduce-scatter.18.cloned.1.call-start = ((), (), s32[]{:S(2)}) async-start(), calls=%async_computation.23 | async-start | bytes 4325376 | tf_op jit(solution)/shard_map/reduce_scatter | solution.py:275
  842.3 445.4 %reduce-scatter.20.cloned.1.call-start = ((), (), s32[]{:S(2)}) async-start(), calls=%async_computation.24 | async-start | bytes 4325376 | tf_op jit(solution)/shard_map/reduce_scatter | solution.py:276
  853.9 575.8 %reduce-scatter.22.cloned.1.call-start = ((), (), s32[]{:S(2)}) async-start(), calls=%async_computation.25 | async-start | bytes 4325376 | tf_op jit(solution)/shard_map/reduce_scatter | solution.py:278
  864.4 706.6 %reduce-scatter.24.cloned.1.call-start = ((), (), s32[]{:S(2)}) async-start(), calls=%async_computation.26 | async-start | bytes 4325376 | tf_op jit(solution)/shard_map/reduce_scatter | solution.py:279
  873.8 838.9 %reduce-scatter.26.cloned.1.call-start = ((), (), s32[]{:S(2)}) async-start(), calls=%async_computation.27 | async-start | bytes 4325376 | tf_op jit(solution)/shard_map/reduce_scatter | solution.py:280
  883.2 971.4 %reduce-scatter.28.cloned.1.call-start = ((), (), s32[]{:S(2)}) async-start(), calls=%async_computation.28 | async-start | bytes 4325376 | tf_op jit(solution)/shard_map/reduce_scatter | solution.py:281
  893.0 1147.4 %reduce-scatter.30.cloned.1.call-start = ((), (), s32[]{:S(2)}) async-start(), calls=%async_computation.29 | async-start | bytes 17301504 | tf_op jit(solution)/shard_map/reduce_scatter | solution.py:229
  923.1 1303.9 %reduce-scatter.32.cloned.1.call-start = ((), (), s32[]{:S(2)}) async-start(), calls=%async_computation.30 | async-start | bytes 17301504 | tf_op jit(solution)/shard_map/reduce_scatter | solution.py:230
  957.4 1403.9 %reduce-scatter.34.cloned.1.call-start = ((), (), s32[]{:S(2)}) async-start(), calls=%async_computation.31 | async-start | bytes 540672
  959.0 9.1 copy-start.2
  959.0 9.1 copy-start.73
  968.1 9.0 copy-start.46
  992.5 46.5 %copy-start.17 = (f32[512,1024]{1,0:T(8,128)S(1)}, f32[512,1024]{1,0:T(8,128)}, u32[]{:S(2)}) copy-start(f32[512,1024]{1,0:T(8,128)} %copy-done.14) | copy-start | bytes 6291460
  (54 other events, 177.1 us)
Sparse Core Ops, SparseCore 0:
  11.0 59.4 all-gather.14
  73.5 55.5 all-gather.10
  132.1 55.3 all-gather.12
  190.3 55.3 all-gather.16
  248.5 55.3 all-gather.18
  306.7 55.3 all-gather.20
  365.0 55.3 all-gather.22
  423.4 55.3 all-gather.24
  481.7 76.2 all-gather.28
  560.9 75.8 all-gather.26
  721.0 141.2 reduce-scatter.13
  864.4 139.6 reduce-scatter.15
  1006.3 139.5 reduce-scatter.17
  1148.1 139.5 reduce-scatter.19
  1289.8 139.8 reduce-scatter.21
  1431.8 139.1 reduce-scatter.23
  1573.1 139.5 reduce-scatter.25
  1714.8 139.7 reduce-scatter.27
  1856.9 183.4 reduce-scatter.29
  2042.6 184.3 reduce-scatter.31
  2229.8 131.4 reduce-scatter.33
where the time goes:
time: 2380 us; the launch traced here: 2370 us
  waiting for transfers between devices  1690 us (71%)
  local copies, waits for them, and re-layouts  232 us (10%)
  matrix products  228 us (10%)
  blocking collectives  123 us (5%)
  other arithmetic  78.5 us (3%)
    reduce_scatter x1, waiting for transfers between devices, on_device(): lax.psum_scatter(to_lanes(grad_wdown), ('dp', 'fsdp'), scatter_dimension=...  185 us
    reduce_scatter x1, waiting for transfers between devices, on_device(): lax.psum_scatter(to_lanes(grad_wup), ('dp', 'fsdp'), scatter_dimension=0,...  184 us
    reduce_scatter x1, waiting for transfers between devices, on_device(): lax.psum_scatter(to_lanes(grad_sq), ('dp', 'fsdp'), scatter_dimension=0,...  140 us
    reduce_scatter x1, waiting for transfers between devices, on_device(): lax.psum_scatter(to_lanes(grad_so), ('dp', 'fsdp'), scatter_dimension=0,...  140 us
    reduce_scatter x1, waiting for transfers between devices, on_device(): lax.psum_scatter(to_lanes(grad_wo), ('dp', 'fsdp'), scatter_dimension=0,...  140 us
    reduce_scatter x1, waiting for transfers between devices, on_device(): lax.psum_scatter(to_lanes(grad_sv), ('dp', 'fsdp'), scatter_dimension=0,...  140 us
    reduce_scatter x1, waiting for transfers between devices, on_device(): lax.psum_scatter(to_lanes(grad_sk), ('dp', 'fsdp'), scatter_dimension=0,...  140 us
    unnamed x22, waiting for transfers between devices  139 us
  transfers between devices with their start and end apart: 21, of which 17 were waited for; matrix products, arithmetic and copies ran while one was open for 18% of the time, Pallas kernels for 0%

commit v1 on v0

v1 whole, which is shorter than its diff:
```python
import functools

import jax
import jax.numpy as jnp
from jax import lax
from jax.experimental import pallas as pl
from jax.experimental.pallas import tpu as pltpu
from jax.sharding import PartitionSpec as P

HEADS = 8
HEAD = 128
D = 1024
FF = 4096
LAT = 128
NEIGH = 512

EPSILON = 1e-05
MASK_FILL = -1e30
SCALE = HEAD**-0.5
GELU_K = 0.7978845608028654
GELU_C = 0.044715

AXES = ("dp", "fsdp")
MESH = pl.DeviceIdType.MESH
F32 = jnp.float32
BF16 = jnp.bfloat16

LINKED_MESH = (4, 8)
PARTS = 32
PART = D // PARTS
SMALL = 256
QUARTERS = FF // D

W_K, W_V, W_Q, W_O, S_Q, S_K, S_V, S_O, UP, DOWN = 0, 1, 2, 3, 4, 5, 6, 7, 8, 12
CHUNKS = 16
TINY = CHUNKS

Y, X, ZH, ZL, CORE = range(5)
STAGES = 5
GATHER_ORDERS = ((ZL, ZH, X, Y, CORE), (ZL, ZH, Y, X, CORE), (ZH, X, Y, ZL, CORE), (ZH, Y, X, ZL, CORE))
GATHER_MIX = (0, 1, 0, 1, 2, 3)
GATHER_LAG = 4
REDUCE_ORDERS = tuple(tuple(reversed(order)) for order in GATHER_ORDERS)
LAND_SLOTS = 3
TERM_SLOTS = 2
WEIGHT_SLOTS = 3
LOADS = tuple(range(CHUNKS)) + tuple(range(UP, DOWN)) + (S_O, S_Q, S_K, S_V, W_O, W_Q, W_K, W_V)
QUEUE = tuple(range(DOWN, CHUNKS)) + tuple(range(UP, DOWN)) + (S_O, S_Q, S_K, S_V, W_O, W_K, W_V, W_Q, TINY)


def dot_nn(left, right):
    return jnp.dot(left, right, preferred_element_type=F32)


def dot_nt(left, right):
    return lax.dot_general(left, right, (((1,), (1,)), ((), ())), preferred_element_type=F32)


def dot_tn(left, right):
    return lax.dot_general(left, right, (((0,), (0,)), ((), ())), preferred_element_type=F32)


def row_mean(rows):
    return jnp.mean(rows, axis=-1, keepdims=True)


def normalised(rows):
    centred = rows - row_mean(rows)
    inv = lax.rsqrt(row_mean(centred * centred) + EPSILON)
    return centred * inv, inv


def norm_back(rows, gain, grad):
    unit, inv = normalised(rows)
    scaled = grad * gain
    pull = inv * (scaled - row_mean(scaled) - unit * row_mean(scaled * unit))
    return pull, jnp.sum(grad * unit, axis=0, keepdims=True), unit


def bits_of():
    row, col = lax.axis_index("dp"), lax.axis_index("fsdp")
    return (row // 2, row % 2, col // 4, (col // 2) % 2, col % 2)


def across(bits, axis):
    other = [1 - bit if at == axis else bit for at, bit in enumerate(bits)]
    return (other[Y] * 2 + other[X], other[ZH] * 4 + other[ZL] * 2 + other[CORE])


class Gather:
    def __init__(self, refs, bits):
        self.refs, self.bits = refs, bits
        self.pieces = [(TINY, 0, PART, GATHER_ORDERS[0])]
        for chunk in range(CHUNKS):
            for half in range(2):
                order = GATHER_ORDERS[GATHER_MIX[(2 * chunk + half) % len(GATHER_MIX)]]
                self.pieces.append((chunk, half * (PART // 2), PART // 2, order))
        self.ticks = len(self.pieces) + STAGES * GATHER_LAG
        self.now, self.done, self.own = 0, 0, False

    def shard(self, chunk, row, rows):
        if chunk == TINY:
            return self.refs["small"].at[pl.ds(row, rows)]
        if chunk < UP:
            return self.refs["attn"][chunk].at[pl.ds(row, rows)]
        if chunk < DOWN:
            return self.refs["up"].at[chunk - UP, pl.ds(row, rows)]
        return self.refs["down"].at[pl.ds((chunk - DOWN) * PART + row, rows)]

    def place(self, chunk, index, row, rows):
        if chunk == TINY:
            return self.refs["full_small"].at[(*index, pl.ds(row, rows))]
        return self.refs["full"].at[(chunk, *index, pl.ds(row, rows))]

    def own_copies(self):
        for chunk in range(CHUNKS + 1):
            yield pltpu.make_async_copy(
                self.shard(chunk, 0, PART), self.place(chunk, self.bits, 0, PART), self.refs["own_sem"].at[chunk]
            )

    def copy(self, piece, stage):
        chunk, row, rows, order = self.pieces[piece]
        if stage == 0:
            source, target = self.shard(chunk, row, rows), self.place(chunk, self.bits, row, rows)
        else:
            index = [pl.ds(0, 2) if axis in order[:stage] else self.bits[axis] for axis in range(5)]
            source = target = self.place(chunk, index, row, rows)
        return pltpu.make_async_remote_copy(
            src_ref=source,
            dst_ref=target,
            send_sem=self.refs["g_send"].at[piece, stage],
            recv_sem=self.refs["g_recv"].at[piece, stage],
            device_id=across(self.bits, order[stage]),
            device_id_type=MESH,
        )

    def start(self):
        for copy in self.own_copies():
            copy.start()

    def tick(self):
        if self.now >= self.ticks:
            return
        for stage in range(STAGES, -1, -1):
            piece = self.now - stage * GATHER_LAG
            if not 0 <= piece < len(self.pieces):
                continue
            if stage > 0:
                if not self.own:
                    self.own = True
                    for copy in self.own_copies():
                        copy.wait()
                self.copy(piece, stage - 1).wait_recv()
            if stage < STAGES:
                self.copy(piece, stage).start()
            else:
                self.done = piece + 1
        self.now += 1

    def need(self, chunk):
        last = 0 if chunk == TINY else 2 * chunk + 2
        while self.done <= last:
            self.tick()

    def finish(self):
        while self.now < self.ticks:
            self.tick()
        for piece in range(len(self.pieces)):
            for stage in range(STAGES):
                self.copy(piece, stage).wait_send()


class Reduce:
    def __init__(self, refs, bits):
        self.refs, self.bits = refs, bits
        self.lands = [refs[f"land{stage}"] for stage in range(STAGES)]
        self.now, self.begun = 0, []

    def pieces(self, at):
        if QUEUE[at] == TINY:
            return [(0, 0, SMALL, REDUCE_ORDERS[0])]
        return [(0, 0, 384, REDUCE_ORDERS[0]), (1, 384, 384, REDUCE_ORDERS[1]), (2, 768, 256, REDUCE_ORDERS[2 + at % 2])]

    def open_axes(self, order, stage):
        return [axis for axis in range(5) if axis not in order[: stage + 1]]

    def kept(self, order, stage, spot):
        return [self.bits[one] if one == order[stage] else spot(one) for one in self.open_axes(order, stage - 1)]

    def copy(self, at, stage, piece):
        number, col, cols, order = piece
        slot, span = at % LAND_SLOTS, pl.ds(col, cols)
        every = pl.ds(0, 2)
        if stage == 0:
            source = self.refs["term"].at[(at % TERM_SLOTS, 1 - self.bits[CORE], *[every] * 4, pl.ds(0, PART), span)]
        else:
            index = [
                1 - self.bits[one] if one == order[stage] else every for one in self.open_axes(order, stage - 1)
            ]
            source = self.lands[stage - 1].at[(slot, *index, pl.ds(0, PART), span)]
        target = self.lands[stage].at[(slot, *[every] * (4 - stage), pl.ds(0, PART), span)]
        return pltpu.make_async_remote_copy(
            src_ref=source,
            dst_ref=target,
            send_sem=self.refs["r_send"].at[at, stage, number],
            recv_sem=self.refs["r_recv"].at[at, stage, number],
            device_id=across(self.bits, order[stage]),
            device_id_type=MESH,
        )

    def credit(self, stage, number, axis):
        return self.refs["credit"].at[stage, number, axis]

    def release(self, at, stage):
        later = at + LAND_SLOTS
        if later >= len(QUEUE):
            return
        for number, _, _, order in self.pieces(later):
            axis = order[stage]
            pl.semaphore_signal(
                self.credit(stage, number, axis), inc=1, device_id=across(self.bits, axis), device_id_type=MESH
            )

    def send(self, at, stage):
        for piece in self.pieces(at):
            if at >= LAND_SLOTS:
                pl.semaphore_wait(self.credit(stage, piece[0], piece[3][stage]), 1)
            self.copy(at, stage, piece).start()

    def add(self, at, stage, piece):
        number, col, cols, order = piece
        slot, span, land = at % LAND_SLOTS, pl.ds(col, cols), self.lands[stage]
        left = self.open_axes(order, stage)

        def step(i, carry):
            index = [(i >> (len(left) - 1 - k)) & 1 for k in range(len(left))]
            if stage == 0:
                extra = self.refs["term"][(at % TERM_SLOTS, self.bits[CORE], *index, slice(None), span)]
            else:
                kept = self.kept(order, stage, dict(zip(left, index)).get)
                extra = self.lands[stage - 1][(slot, *kept, slice(None), span)]
            land[(slot, *index, slice(None), span)] += extra
            return carry

        lax.fori_loop(0, 1 << len(left), step, 0)

    def advance(self, at, stage):
        pieces = self.pieces(at)
        last = stage == STAGES
        slot = at % LAND_SLOTS
        if last:
            self.final_ready(at)
        for piece in pieces:
            self.copy(at, stage - 1, piece).wait_recv()
        if stage == 1:
            self.add(at, 0, (0, 0, SMALL if QUEUE[at] == TINY else D, pieces[0][3]))
        else:
            for piece in pieces:
                if last:
                    _, col, cols, order = piece
                    span = pl.ds(col, cols)
                    mine = self.lands[3][(slot, *self.kept(order, 4, None), slice(None), span)]
                    came = self.lands[4][slot, :, span]
                    self.refs["final"][at % 2, :, span] = mine.astype(F32) + came.astype(F32)
                else:
                    self.add(at, stage - 1, piece)
        if last:
            self.final_copy(at).start()
        else:
            self.send(at, stage)
        for piece in pieces:
            self.copy(at, stage - 1, piece).wait_send()
        if stage >= 2:
            self.release(at, stage - 2)
        if last:
            self.release(at, 4)

    def final_copy(self, at):
        chunk = QUEUE[at]
        source, sem = self.refs["final"].at[at % 2], self.refs["final_sem"].at[at % 2]
        if chunk == TINY:
            source, target = source.at[:, pl.ds(0, SMALL)], self.refs["g_small"]
        elif chunk < UP:
            target = self.refs["g_attn"][chunk]
        elif chunk < DOWN:
            target = self.refs["g_up"].at[chunk - UP]
        else:
            target = self.refs["g_down"].at[pl.ds((chunk - DOWN) * PART, PART)]
        return pltpu.make_async_copy(source, target, sem)

    def final_ready(self, at):
        if at >= 2:
            self.final_copy(at - 2).wait()

    def tick(self, tile):
        for at, began in enumerate(self.begun):
            if 1 <= self.now - began <= STAGES:
                self.advance(at, self.now - began)
        if tile is not None and len(self.begun) < len(QUEUE):
            at = len(self.begun)
            width = SMALL if QUEUE[at] == TINY else D
            for i in range(2):
                value = tile(QUEUE[at], i).astype(BF16).reshape(8, 2, PART, width)
                for core in range(2):
                    for j in range(8):
                        index = (at % TERM_SLOTS, core, i, j >> 2, (j >> 1) & 1, j & 1, slice(None), pl.ds(0, width))
                        self.refs["term"][index] = value[j, core]
            self.send(at, 0)
            self.begun.append(self.now)
        self.now += 1

    def finish(self):
        assert len(self.begun) == len(QUEUE)
        while self.now - self.begun[-1] <= STAGES:
            self.tick(None)
        for at in (len(QUEUE) - 2, len(QUEUE) - 1):
            self.final_copy(at).wait()


class Local:
    def __init__(self, refs):
        self.refs, self.count, self.tiles = refs, 0, 0

    def copy(self, tile):
        chunk, half = QUEUE[tile // 2], tile % 2
        rows = pl.ds(half * 512, 512)
        if chunk < UP:
            target = self.refs["g_attn"][chunk].at[rows]
        elif chunk < DOWN:
            target = self.refs["g_up"].at[chunk - UP, rows]
        else:
            target = self.refs["g_down"].at[pl.ds((chunk - DOWN) * D + half * 512, 512)]
        return pltpu.make_async_copy(self.refs["term"].at[half], target, self.refs["term_sem"].at[half])

    def tick(self, tile):
        if tile is None or self.count >= len(QUEUE):
            return
        chunk = QUEUE[self.count]
        self.count += 1
        for half in range(2):
            value = tile(chunk, half)
            if chunk == TINY:
                self.refs["g_small"][pl.ds(half * 512, 512), :] = value
                continue
            if self.tiles >= 2:
                self.copy(self.tiles - 2).wait()
            self.refs["term"][half] = value.astype(BF16)
            self.copy(self.tiles).start()
            self.tiles += 1

    def finish(self):
        assert self.count == len(QUEUE)
        for tile in (self.tiles - 2, self.tiles - 1):
            self.copy(tile).wait()


class Weights:
    def __init__(self, refs, gather):
        self.refs, self.gather = refs, gather
        self.fetched, self.used = 0, 0

    def copy(self, at):
        chunk = LOADS[at]
        if self.gather is not None:
            source = self.refs["full"].at[chunk]
        elif chunk < UP:
            source = self.refs["attn"][chunk]
        elif chunk < DOWN:
            source = self.refs["up"].at[chunk - UP]
        else:
            source = self.refs["down"].at[chunk - DOWN]
        slot = at % WEIGHT_SLOTS
        return pltpu.make_async_copy(source, self.refs["held"].at[slot], self.refs["held_sem"].at[slot])

    def fetch(self, limit):
        while self.fetched < min(limit, len(LOADS)):
            if self.gather is not None:
                self.gather.need(LOADS[self.fetched])
            self.copy(self.fetched).start()
            self.fetched += 1

    def use(self, chunk, keep=0):
        at = self.used
        assert LOADS[at] == chunk
        self.fetch(at + 1)
        if at >= CHUNKS:
            self.fetch(at + WEIGHT_SLOTS - keep)
        self.copy(at).wait()
        self.used += 1
        return lambda: self.refs["held"][at % WEIGHT_SLOTS].reshape(D, D)


NAMES_IN = ("small", "w_k", "w_v", "w_q", "w_o", "s_q", "s_k", "s_v", "s_o", "up", "down", "points", "near", "lens", "cot")
NAMES_OUT = ("out", "point_grad", "g_small", "g_k", "g_v", "g_q", "g_o", "gs_q", "gs_k", "gs_v", "gs_o", "g_up", "g_down")


def layer_kernel(linked, names, *refs):
    r = dict(zip(names, refs, strict=True))
    r["attn"] = [r[name] for name in NAMES_IN[1:9]]
    r["g_attn"] = [r[name] for name in NAMES_OUT[3:11]]
    points, near, lens, cot = r["points"], r["near"], r["lens"], r["cot"]
    keys, values, wide, slope = r["keys"], r["values"], r["wide"], r["slope"]
    cross_mix, self_mix, h_s, h_m = r["cross_mix"], r["self_mix"], r["h_s"], r["h_m"]
    self_q, self_k, self_v = r["self_q"], r["self_k"], r["self_v"]
    two_low, one_low, mix_grad = r["two_low"], r["one_low"], r["mix_grad"]
    res_one, res_two, grad, part = r["res_one"], r["res_two"], r["grad"], r["part"]
    scores, score_grad, lat, lat_grad = r["scores"], r["score_grad"], r["lat"], r["lat_grad"]
    h_q, query, lse, gains, gain_grads = r["h_q"], r["query"], r["lse"], r["gains"], r["gain_grads"]
    count_log = r["count_log"]
    groups = near.shape[0]
    rows, slots = cot.shape[0], keys.shape[0]
    half = slots // 2

    if linked:
        bits = bits_of()
        barrier = pltpu.get_barrier_semaphore()
        for axis in range(5):
            pl.semaphore_signal(barrier, inc=1, device_id=across(bits, axis), device_id_type=MESH)
        pl.semaphore_wait(barrier, 5)
        gather, reduce = Gather(r, bits), Reduce(r, bits)
        gather.start()
        move = gather.tick
    else:
        gather, reduce = None, Local(r)
        move = lambda: None
    weights = Weights(r, gather)

    point_load = pltpu.make_async_copy(points, slope, r["point_sem"].at[0])
    point_load.start()
    for _ in range(8):
        move()

    for g in range(groups):
        listed = near[pl.ds(g, 1), :]
        live = lax.broadcasted_iota(jnp.int32, (1, NEIGH), 1) < lens[g]
        high = lax.broadcasted_iota(jnp.int32, (slots // 128, NEIGH), 0) == listed // 128
        low = lax.broadcasted_iota(jnp.int32, (128, NEIGH), 0) == listed % 128
        high = jnp.where(high & live, 1.0, 0.0).astype(BF16)
        low = jnp.where(low, 1.0, 0.0).astype(BF16)
        count = dot_nt(high, low)
        count = jnp.where(count > 0.5, jnp.log(jnp.maximum(count, 1.0)), MASK_FILL)
        for a in range(slots // 128):
            count_log[pl.ds(g, 1), pl.ds(a * 128, 128)] = count[a : a + 1, :]

    if linked:
        gather.need(TINY)
        small_load = pltpu.make_async_copy(r["full_small"], r["small_in"], r["tiny_sem"].at[0])
    else:
        small_load = pltpu.make_async_copy(r["small"], r["small_in"], r["tiny_sem"].at[0])
    small_load.start()
    small_load.wait()
    turned = r["small_in"][...].reshape(D, SMALL).astype(F32).T
    lat[...] = turned[:LAT]
    gains[...] = turned[LAT : LAT + 8]
    gain_grads[...] = jnp.zeros_like(gain_grads)
    gain_of = lambda i: gains[pl.ds(i, 1), :]
    h_q[...] = (normalised(lat[...])[0] * gain_of(0)).astype(BF16)
    point_load.wait()

    tile = 64

    def span_of(i, size=tile):
        return pl.ds(pl.multiple_of(i * size, size), size)

    def head_of(h):
        return pl.ds(pl.multiple_of(h * HEAD, HEAD), HEAD)

    def each(count, step):
        def body(i, carry):
            step(i)
            return carry

        lax.fori_loop(0, count, body, 0)

    def norm_points(i):
        at = span_of(i)
        wide[at, :] = (normalised(slope[at, :].astype(F32))[0] * gain_of(1)).astype(BF16)

    each(slots // tile, norm_points)

    for chunk, target in ((W_K, keys), (W_V, values)):
        w = weights.use(chunk)

        def project(i, target=target, w=w):
            at = span_of(i, 512)
            target[at, :] = dot_nn(wide[at, :], w()).astype(BF16)

        each(slots // 512, project)
        move()
    w = weights.use(W_Q)
    query[...] = dot_nn(h_q[...], w()).astype(BF16)

    lane = lax.broadcasted_iota(jnp.int32, (LAT, HEAD), 1)

    def weigh(h):
        hs = head_of(h)
        scores[...] = dot_nt(query[:, hs], keys[:, hs]) * SCALE
        for g in range(groups):
            def softmax(i, g=g):
                at = span_of(i, 32)
                logit = scores[at, :] + count_log[pl.ds(g, 1), :]
                top = jnp.max(logit, axis=-1, keepdims=True)
                terms = jnp.exp(logit - top)
                total = jnp.sum(terms, axis=-1, keepdims=True)
                probs = (terms / total).astype(BF16)
                row = pl.ds(pl.multiple_of(g * LAT + i * 32, 32), 32)
                wide[row, :] = probs[:, :half]
                wide[pl.ds(pl.multiple_of(rows + g * LAT + i * 32, 32), 32), :] = probs[:, half:]
                here = lax.broadcasted_iota(jnp.int32, (32, HEAD), 1) == h
                lse[row, :] = jnp.where(here, top + jnp.log(total), lse[row, :])

            each(LAT // 32, softmax)
        mixed = dot_nn(wide[pl.ds(0, rows), :], values[pl.ds(0, half), hs])
        mixed += dot_nn(wide[pl.ds(rows, rows), :], values[pl.ds(half, half), hs])
        cross_mix[:, hs] = mixed.astype(BF16)

    lse[...] = jnp.zeros_like(lse)
    for part_at in range(4):
        each(2, lambda i, part_at=part_at: weigh(part_at * 2 + i))
        move()
        move()

    w = weights.use(W_O)
    res_one[...] = dot_nn(cross_mix[...], w())

    def add_latents(i):
        at = span_of(i)
        total = res_one[at, :] + lat[span_of(i % (LAT // tile)), :]
        res_one[at, :] = total
        h_s[at, :] = (normalised(total)[0] * gain_of(2)).astype(BF16)

    each(rows // tile, add_latents)
    for chunk, target in ((S_Q, self_q), (S_K, self_k), (S_V, self_v)):
        w = weights.use(chunk)
        target[...] = dot_nn(h_s[...], w()).astype(BF16)

    def group_of(g):
        return pl.ds(g * LAT, LAT)

    def self_probs(g, hs):
        logit = dot_nt(self_q[group_of(g), hs], self_k[group_of(g), hs]) * SCALE
        terms = jnp.exp(logit - jnp.max(logit, axis=-1, keepdims=True))
        return terms / jnp.sum(terms, axis=-1, keepdims=True)

    def self_attend(h):
        hs = head_of(h)
        for g in range(groups):
            probs = self_probs(g, hs).astype(BF16)
            self_mix[group_of(g), hs] = dot_nn(probs, self_v[group_of(g), hs]).astype(BF16)

    each(HEADS, self_attend)
    w = weights.use(S_O)
    res_two[...] = dot_nn(self_mix[...], w())

    def add_first(i):
        at = span_of(i)
        total = res_two[at, :] + res_one[at, :]
        res_two[at, :] = total
        h_m[at, :] = (normalised(total)[0] * gain_of(3)).astype(BF16)

    each(rows // tile, add_first)

    for q in range(QUARTERS):
        w = weights.use(UP + q)

        def expand(i, q=q, w=w):
            u = dot_nn(h_m[span_of(i, 256), :], w())
            square = u * u
            bent = jnp.tanh(GELU_K * (u + GELU_C * square * u))
            at = pl.ds(pl.multiple_of(q * rows + i * 256, 256), 256)
            wide[at, :] = (0.5 * u * (1.0 + bent)).astype(BF16)
            rise = GELU_K * (1.0 + 3.0 * GELU_C * square)
            slope[at, :] = (0.5 * (1.0 + bent) + 0.5 * u * (1.0 - bent * bent) * rise).astype(BF16)

        each(rows // 256, expand)

    def quarter(q):
        return pl.ds(q * rows, rows)

    def terms_of(chunk, i):
        cols = pl.ds(i * 512, 512)
        if chunk == TINY:
            tall = jnp.concatenate((lat_grad[...], gain_grads[...], jnp.zeros((SMALL - LAT - 8, D), F32)), axis=0)
            return tall[:, i * 512 : (i + 1) * 512].T
        if chunk >= DOWN:
            q = chunk - DOWN
            return dot_tn(wide[quarter(q), cols], cot[...])
        if chunk >= UP:
            return dot_tn(h_m[:, cols], slope[quarter(chunk - UP), :])
        left, right = {
            S_O: (self_mix, two_low),
            S_Q: (h_s, self_q),
            S_K: (h_s, self_k),
            S_V: (h_s, self_v),
            W_O: (cross_mix, one_low),
            W_K: (wide, keys),
            W_V: (wide, values),
            W_Q: (h_q, query),
        }[chunk]
        return dot_tn(left[:, cols], right[...])

    def turn(fresh=True):
        reduce.tick(terms_of if fresh else None)

    for q in range(QUARTERS):
        w = weights.use(DOWN + q)
        made = dot_nn(wide[quarter(q), :], w())
        part[...] = made + (res_two[...] if q == 0 else part[...])
        act_grad = dot_nt(cot[...], w())
        slope[quarter(q), :] = (slope[quarter(q), :].astype(F32) * act_grad).astype(BF16)
        turn()
    r["out"][...] = part[...].astype(BF16)
    if linked:
        gather.finish()

    for q in range(QUARTERS):
        w = weights.use(UP + q)
        made = dot_nt(slope[quarter(q), :], w())
        grad[...] = made if q == 0 else grad[...] + made
        if q % 2 == 1:
            turn()

    def gain_add(i, value):
        gain_grads[pl.ds(i, 1), :] += value

    def back_two(i):
        at = span_of(i)
        pull, gain_part, _ = norm_back(res_two[at, :], gain_of(3), grad[at, :])
        total = cot[at, :].astype(F32) + pull
        grad[at, :] = total
        two_low[at, :] = total.astype(BF16)
        gain_add(3, gain_part)

    each(rows // tile, back_two)
    turn()
    w = weights.use(S_O)
    mix_grad[...] = dot_nt(two_low[...], w()).astype(BF16)

    def self_back(h):
        hs = head_of(h)
        for g in range(groups):
            at = group_of(g)
            probs = self_probs(g, hs)
            given = mix_grad[at, hs]
            queries, keyed, valued = self_q[at, hs], self_k[at, hs], self_v[at, hs]
            prob_grad = dot_nt(given, valued)
            inner = jnp.sum(probs * prob_grad, axis=-1, keepdims=True)
            logit_grad = (probs * (prob_grad - inner)).astype(BF16)
            self_q[at, hs] = (dot_nn(logit_grad, keyed) * SCALE).astype(BF16)
            self_k[at, hs] = (dot_tn(logit_grad, queries) * SCALE).astype(BF16)
            self_v[at, hs] = dot_tn(probs.astype(BF16), given).astype(BF16)

    each(HEADS // 2, self_back)
    turn()
    each(HEADS // 2, lambda i: self_back(HEADS // 2 + i))
    turn()
    w = weights.use(S_Q)
    part[...] = dot_nt(self_q[...], w())
    w = weights.use(S_K)
    part[...] += dot_nt(self_k[...], w())
    w = weights.use(S_V)
    part[...] += dot_nt(self_v[...], w())

    def back_one(i):
        at = span_of(i)
        pull, gain_part, _ = norm_back(res_one[at, :], gain_of(2), part[at, :])
        total = grad[at, :] + pull
        grad[at, :] = total
        one_low[at, :] = total.astype(BF16)
        gain_add(2, gain_part)

    each(rows // tile, back_one)
    turn()

    def sum_groups(i):
        total = grad[span_of(i), :]
        for g in range(1, groups):
            total += grad[pl.ds(pl.multiple_of(g * LAT + i * tile, tile), tile), :]
        lat_grad[span_of(i), :] = total

    each(LAT // tile, sum_groups)
    w = weights.use(W_O)
    mix_grad[...] = dot_nt(one_low[...], w()).astype(BF16)

    def cross_back(h):
        hs = head_of(h)
        scores[...] = dot_nt(query[:, hs], keys[:, hs]) * SCALE
        for g in range(groups):
            res_two_view = dot_nt(mix_grad[group_of(g), hs], values[:, hs])
            part[pl.ds(0, LAT), :] = res_two_view[:, :half]
            part[pl.ds(LAT, LAT), :] = res_two_view[:, half:]

            def softmax_back(i, g=g):
                at = span_of(i, 32)
                row = pl.ds(pl.multiple_of(g * LAT + i * 32, 32), 32)
                here = lax.broadcasted_iota(jnp.int32, (32, HEAD), 1) == h
                total = jnp.sum(jnp.where(here, lse[row, :], 0.0), axis=-1, keepdims=True)
                low_row = pl.ds(pl.multiple_of(LAT + i * 32, 32), 32)
                prob_grads = (part[at, :], part[low_row, :])
                probs, inner = [], 0.0
                for side in range(2):
                    cols = pl.ds(side * half, half)
                    prob = jnp.exp(scores[at, cols] + count_log[pl.ds(g, 1), cols] - total)
                    wide[pl.ds(pl.multiple_of(side * rows + g * LAT + i * 32, 32), 32), :] = prob.astype(BF16)
                    inner += jnp.sum(prob * prob_grads[side], axis=-1, keepdims=True)
                    probs.append(prob)
                for side in range(2):
                    cols = pl.ds(side * half, half)
                    made = probs[side] * (prob_grads[side] - inner)
                    score_grad[at, cols] = made if g == 0 else score_grad[at, cols] + made

            each(LAT // 32, softmax_back)
        logit_grad = score_grad[...].astype(BF16)
        asked = query[:, hs]
        query_back = dot_nn(logit_grad, keys[:, hs]) * SCALE
        keys[:, hs] = (dot_tn(logit_grad, asked) * SCALE).astype(BF16)
        query[:, hs] = query_back.astype(BF16)
        for side in range(2):
            probs = wide[pl.ds(side * rows, rows), :]
            values[pl.ds(side * half, half), hs] = dot_tn(probs, mix_grad[:, hs]).astype(BF16)

    point_load.start()
    for part_at in range(4):
        each(2, lambda i, part_at=part_at: cross_back(part_at * 2 + i))
        turn(part_at < 3)

    w = weights.use(W_Q)
    pull, gain_part, _ = norm_back(lat[...], gain_of(0), dot_nt(query[...], w()))
    lat_grad[...] += pull
    gain_add(0, gain_part)

    point_load.wait()
    each(slots // tile, norm_points)
    turn()
    w_keys, w_values = weights.use(W_K), weights.use(W_V, keep=1)
    point_stores = []
    for block in range(slots // 512):
        at = pl.ds(block * 512, 512)
        part[...] = dot_nt(keys[at, :], w_keys()) + dot_nt(values[at, :], w_values())

        def back_points(i, block=block):
            row = pl.ds(pl.multiple_of(block * 512 + i * tile, tile), tile)
            pull, gain_part, _ = norm_back(slope[row, :].astype(F32), gain_of(1), part[span_of(i), :])
            slope[row, :] = pull.astype(BF16)
            gain_add(1, gain_part)

        each(512 // tile, back_points)
        store = pltpu.make_async_copy(slope.at[at], r["point_grad"].at[at], r["point_sem"].at[block])
        store.start()
        point_stores.append(store)
        if block < 2:
            turn()
    while len(getattr(reduce, "begun", ())) < len(QUEUE) and linked or not linked and reduce.count < len(QUEUE):
        turn()
    reduce.finish()
    for store in point_stores:
        store.wait()


def layer_call(linked, small, attn, up, down, points, near, lens, cot):
    slots, rows, groups = points.shape[0], cot.shape[0], near.shape[0]
    any_space = pl.BlockSpec(memory_space=pl.ANY)
    in_vmem = pl.BlockSpec(memory_space=pltpu.VMEM)
    in_smem = pl.BlockSpec(memory_space=pltpu.SMEM)
    shape = jax.ShapeDtypeStruct
    split = (2,) * 5
    outs = [shape((rows, D), BF16), shape((slots, D), BF16)]
    out_specs = [in_vmem, any_space]
    if linked:
        outs += [shape((PART, SMALL), F32)] + [shape((PART, D), F32)] * 8
        outs += [shape((QUARTERS, PART, D), F32), shape((QUARTERS * PART, D), F32)]
        out_specs += [any_space] * 11
        outs += [shape((CHUNKS, *split, PART, D), BF16), shape((*split, PART, SMALL), BF16)]
        out_specs += [any_space] * 2
    else:
        outs += [shape((D, SMALL), F32)] + [shape((D, D), BF16)] * 8
        outs += [shape((QUARTERS, D, D), BF16), shape((FF, D), BF16)]
        out_specs += [in_vmem] + [any_space] * 10
    vmem, dma = pltpu.VMEM, pltpu.SemaphoreType.DMA
    scratch = {
        "keys": vmem((slots, D), BF16),
        "values": vmem((slots, D), BF16),
        "wide": vmem((QUARTERS * rows, D), BF16),
        "slope": vmem((QUARTERS * rows, D), BF16),
    }
    for name in ("cross_mix", "self_mix", "h_s", "h_m", "self_q", "self_k", "self_v", "two_low", "one_low", "mix_grad"):
        scratch[name] = vmem((rows, D), BF16)
    for name in ("res_one", "res_two", "grad", "part"):
        scratch[name] = vmem((rows, D), F32)
    scratch |= {
        "scores": vmem((LAT, slots), F32),
        "score_grad": vmem((LAT, slots), F32),
        "lat": vmem((LAT, D), F32),
        "lat_grad": vmem((LAT, D), F32),
        "h_q": vmem((LAT, D), BF16),
        "query": vmem((LAT, D), BF16),
        "lse": vmem((rows, HEAD), F32),
        "gains": vmem((8, D), F32),
        "gain_grads": vmem((8, D), F32),
        "small_in": vmem((*split, PART, SMALL), BF16),
        "count_log": vmem((groups, slots), F32),
        "held": vmem((WEIGHT_SLOTS, *split, PART, D), BF16),
        "held_sem": dma((WEIGHT_SLOTS,)),
        "point_sem": dma((slots // 512,)),
        "tiny_sem": dma((1,)),
    }
    if linked:
        scratch["term"] = vmem((TERM_SLOTS, 2, 2, 2, 2, 2, PART, D), BF16)
        for stage in range(STAGES):
            scratch[f"land{stage}"] = vmem((LAND_SLOTS, *(2,) * (4 - stage), PART, D), BF16)
        pieces = 2 * CHUNKS + 1
        scratch |= {
            "final": vmem((2, PART, D), F32),
            "g_send": dma((pieces, STAGES)),
            "g_recv": dma((pieces, STAGES)),
            "own_sem": dma((CHUNKS + 1,)),
            "r_send": dma((len(QUEUE), STAGES, 3)),
            "r_recv": dma((len(QUEUE), STAGES, 3)),
            "credit": pltpu.SemaphoreType.REGULAR((STAGES, 3, 5)),
            "final_sem": dma((2,)),
        }
    else:
        scratch |= {"term": vmem((2, 512, D), BF16), "term_sem": dma((2,))}
    names = NAMES_IN + NAMES_OUT + (("full", "full_small") if linked else ()) + tuple(scratch)
    params = {"collective_id": 0} if linked else {}
    return pl.pallas_call(
        functools.partial(layer_kernel, linked, names),
        out_shape=outs,
        in_specs=[any_space] * 12 + [in_vmem, in_smem, in_vmem],
        out_specs=out_specs,
        scratch_shapes=list(scratch.values()),
        compiler_params=pltpu.CompilerParams(has_side_effects=True, vmem_limit_bytes=63 << 20, **params),
    )(small, *attn, up, down, points, near, lens, cot)


def on_device(
    linked, latents, gain_q, gain_kv, w_q, w_k, w_v, w_o, gain_s, s_q, s_k, s_v, s_o, gain_m, w_up, w_down,
    points, neighbours, lengths, cotangent,
):
    own = latents.shape[1]
    split = (2,) * 5
    small = jnp.concatenate((latents, jnp.stack((gain_q, gain_kv, gain_s, gain_m))), axis=0)
    small = jnp.pad(small.T, ((0, 0), (0, SMALL - LAT - 4)))
    attn = (w_k, w_v, w_q, w_o, s_q, s_k, s_v, s_o)
    if linked:
        up = w_up.reshape(own, PARTS, QUARTERS, PART).transpose(2, 0, 1, 3).reshape(QUARTERS, own, D)
        made = layer_call(True, small, attn, up, w_down, points, neighbours, lengths, cotangent)[: len(NAMES_OUT)]
        out, point_grad, g_small, g_k, g_v, g_q, g_o, gs_q, gs_k, gs_v, gs_o, g_up, g_down = made
        g_up = g_up.reshape(QUARTERS, own, PARTS, PART).transpose(1, 2, 0, 3).reshape(own, FF)
    else:
        gathered = lambda shard: lax.all_gather(shard, AXES, axis=0, tiled=True)
        blocks = lambda whole: whole.reshape(*split, PART, whole.shape[-1])
        up = gathered(w_up).reshape(D, QUARTERS, D).transpose(1, 0, 2).reshape(QUARTERS, *split, PART, D)
        down = gathered(w_down).reshape(QUARTERS, *split, PART, D)
        made = layer_call(
            False, blocks(gathered(small)), [blocks(gathered(one)) for one in attn], up, down,
            points, neighbours, lengths, cotangent,
        )
        out, point_grad = made[:2]
        summed = lambda whole: lax.psum_scatter(whole.astype(F32), AXES, scatter_dimension=0, tiled=True)
        g_small, g_k, g_v, g_q, g_o, gs_q, gs_k, gs_v, gs_o = [summed(one) for one in made[2:11]]
        g_up = summed(made[11].transpose(1, 0, 2).reshape(D, FF))
        g_down = summed(made[12])
    turned = g_small.T
    return (
        out, point_grad, turned[:LAT], turned[LAT], turned[LAT + 1], g_q, g_k, g_v, g_o,
        turned[LAT + 2], gs_q, gs_k, gs_v, gs_o, turned[LAT + 3], g_up, g_down,
    )


def solution(mesh):
    linked = (mesh.shape["dp"], mesh.shape["fsdp"]) == LINKED_MESH
    row, vector, matrix = P(None, AXES), P(AXES), P(AXES, None)
    return jax.shard_map(
        functools.partial(on_device, linked),
        mesh=mesh,
        in_specs=(
            row, vector, vector, matrix, matrix, matrix, matrix, vector, matrix, matrix, matrix, matrix, vector,
            matrix, matrix, matrix, matrix, vector, matrix,
        ),
        out_specs=(
            matrix, matrix, row, vector, vector, matrix, matrix, matrix, matrix,
            vector, matrix, matrix, matrix, matrix, vector, matrix, matrix,
        ),
        check_vma=False,
    )
```

time: 2380 us -> 452 us (0.19)
  waiting for transfers between devices: 1690 us -> 0 us
  Pallas kernels: 0 us -> 415 us
  matrix products: 228 us -> 0 us
  local copies, waits for them, and re-layouts: 232 us -> 32.2 us
  blocking collectives: 123 us -> 0 us
  other arithmetic: 78.5 us -> 0 us
    reduce_scatter x10 -> x0, waiting for transfers between devices: 1160 us -> none  [the longest x1 185 us: on_device(): lax.psum_scatter(to_lanes(grad_wdown), ('dp', 'fsdp'), scatter_dimension=...]
    pallas_call x0 -> x1, Pallas kernels: none -> 415 us  [layer_call(): pl.pallas_call(functools.partial(layer_kernel, linked, names), out_shape=...]
    all_gather x10 -> x0, waiting for transfers between devices: 389 us -> none  [the longest x1 74.3 us: on_device(): lax.all_gather(w_down, ('dp', 'fsdp'), axis=0, tiled=True)]
    dot_general x41 -> x0, matrix products: 224 us -> none  [the longest x10 67.7 us: dot_fwd(): return jnp.dot(left_op, right_op, preferred_element_type=jnp.float32)]
    unnamed x22 -> x0, waiting for transfers between devices: 139 us -> none
    reshape x26 -> x5, local copies, waits for them, and re-layouts: 122 us -> 9.93 us  [the longest x2 6.24 us: on_device(): g_up.reshape(QUARTERS, own, PARTS, PART).transpose(1, 2, 0, 3)]
    unnamed x2 -> x0, blocking collectives: 81.8 us -> none
    all_gather x1 -> x0, blocking collectives: 41.5 us -> none  [on_device(): lax.all_gather(latents, ('dp', 'fsdp'), axis=1, tiled=True)]
  transfers between devices with their start and end apart: 21 -> 0, of which waited for: 17 -> 0; matrix products, arithmetic and copies ran while one was open for 18% -> 0% of each run, Pallas kernels for 0% -> 0%
where the time goes in v1:
time: 452 us; the launch traced here: 448 us
  Pallas kernels  415 us (92%)
  local copies, waits for them, and re-layouts  32.2 us (7%)
    pallas_call x1, Pallas kernels, layer_call(): pl.pallas_call(functools.partial(layer_kernel, linked, names), out_shape=...  415 us
    unnamed x31, local copies, waits for them, and re-layouts  11.8 us

profile of v1, /device:TPU:0, one launch (start us, length us, event | category | flops | bytes accessed | tf_op | source)
XLA Modules:
  0.0 447.9 jit_solution(16640425769095516397)
XLA Ops:
  0.7 0.8 copy.42
  1.4 0.8 copy.43
  2.2 0.8 copy.44
  2.9 0.8 copy.45
  3.7 0.8 concatenate.3
  4.4 0.6 pad.4.refs_0_
  5.1 1.7 reshape.46
  6.8 0.2 copy.49
  7.0 1.8 reshape.47.refs_9_
  8.8 414.8 %shard_map.314 = (bf16[512,1024]{1,0:T(8,128)(2,1)}, bf16[2048,1024]{1,0:T(8,128)(2,1)}, f32[32,256]{1,0:T(8,128)}, f32[32,1024]{1,0:T(8,128)}, f32[32,1024]{1,0...) custom-call(bf16[32,256]{1,0:T(8,128)(2,1)} %pad.4.refs_0_, ...), custom_call_target="tpu_custom_call" | custom-call | tf_op jit(solution)/shard_map/pallas_call | solution.py:826
  423.5 1.7 slice_reduce_fusion
  425.2 1.3 slice.20
  426.5 0.0 copy-start
  426.5 1.8 reshape.48
  428.4 3.1 copy.47
  431.5 4.4 reshape.49
  435.9 0.0 copy-done
  435.9 1.0 copy.61
  436.9 0.0 copy-start.9
  436.9 0.0 copy-start.8
  436.9 0.0 copy-start.7
  436.9 0.0 copy-start.6
  436.9 0.0 copy-start.5
  436.9 0.0 copy-start.4
  436.9 0.0 copy-start.3
  436.9 0.0 copy-start.2
  436.9 0.0 copy-start.1
  436.9 4.8 %copy.62 = bf16[2048,1024]{1,0:T(8,128)(2,1)} copy(bf16[2048,1024]{1,0:T(8,128)(2,1)} %get-tuple-element.65) | data formatting | bytes 8388608
  441.7 0.0 copy-done.9
  441.7 0.7 copy.63
  442.3 0.0 copy-done.8
  442.3 0.7 copy.64
  443.0 0.0 copy-done.7
  443.0 0.7 copy.65
  443.7 0.0 copy-done.6
  443.7 0.7 copy.66
  444.3 0.0 copy-done.5
  444.3 0.7 copy.67
  445.0 0.0 copy-done.4
  445.0 0.7 copy.68
  445.6 0.0 copy-done.3
  445.6 0.7 copy.69
  446.3 0.0 copy-done.2
  446.3 0.7 copy.70
  446.9 0.0 copy-done.1
  447.0 0.8 copy.71
Async XLA Ops:
  426.5 9.4 %copy-start = (bf16[512,1024]{1,0:T(8,128)(2,1)S(1)}, bf16[512,1024]{1,0:T(8,128)(2,1)}, u32[]{:S(2)}) copy-start(bf16[512,1024]{1,0:T(8,128)(2,1)} %get-tuple-element.64) | copy-start | bytes 3145732
  436.9 4.8 %copy-start.9 = (f32[32,1024]{1,0:T(8,128)S(1)}, f32[32,1024]{1,0:T(8,128)}, u32[]{:S(2)}) copy-start(f32[32,1024]{1,0:T(8,128)} %get-tuple-element.69) | copy-start | bytes 393220
  436.9 5.5 %copy-start.8 = (f32[32,1024]{1,0:T(8,128)S(1)}, f32[32,1024]{1,0:T(8,128)}, u32[]{:S(2)}) copy-start(f32[32,1024]{1,0:T(8,128)} %get-tuple-element.70) | copy-start | bytes 393220
  436.9 6.1 %copy-start.7 = (f32[32,1024]{1,0:T(8,128)S(1)}, f32[32,1024]{1,0:T(8,128)}, u32[]{:S(2)}) copy-start(f32[32,1024]{1,0:T(8,128)} %get-tuple-element.71) | copy-start | bytes 393220
  436.9 6.8 %copy-start.6 = (f32[32,1024]{1,0:T(8,128)S(1)}, f32[32,1024]{1,0:T(8,128)}, u32[]{:S(2)}) copy-start(f32[32,1024]{1,0:T(8,128)} %get-tuple-element.72) | copy-start | bytes 393220
  436.9 7.4 %copy-start.5 = (f32[32,1024]{1,0:T(8,128)S(1)}, f32[32,1024]{1,0:T(8,128)}, u32[]{:S(2)}) copy-start(f32[32,1024]{1,0:T(8,128)} %get-tuple-element.74) | copy-start | bytes 393220
  436.9 8.1 %copy-start.4 = (f32[32,1024]{1,0:T(8,128)S(1)}, f32[32,1024]{1,0:T(8,128)}, u32[]{:S(2)}) copy-start(f32[32,1024]{1,0:T(8,128)} %get-tuple-element.75) | copy-start | bytes 393220
  436.9 8.7 %copy-start.3 = (f32[32,1024]{1,0:T(8,128)S(1)}, f32[32,1024]{1,0:T(8,128)}, u32[]{:S(2)}) copy-start(f32[32,1024]{1,0:T(8,128)} %get-tuple-element.76) | copy-start | bytes 393220
  436.9 9.4 %copy-start.2 = (f32[32,1024]{1,0:T(8,128)S(1)}, f32[32,1024]{1,0:T(8,128)}, u32[]{:S(2)}) copy-start(f32[32,1024]{1,0:T(8,128)} %get-tuple-element.77) | copy-start | bytes 393220
  436.9 10.0 %copy-start.1 = (f32[128,1024]{1,0:T(8,128)S(1)}, f32[128,1024]{1,0:T(8,128)}, u32[]{:S(2)}) copy-start(f32[128,1024]{1,0:T(8,128)} %get-tuple-element.80) | copy-start | bytes 1572868
